TPU v7x, 256 devices: a whole 4x4x8 slice. The times are simulated.
256 devices in a mesh: client: 32 (over x, z_lo, y), row: 8 (over z_hi, core).
Axes of the slice: x: 4, y: 4, z: 8 (z_hi: 4, z_lo: 2; z = z_hi * 2 + z_lo), core: 2. Of those that a mesh axis runs over, the one named last changes fastest.
Arguments:
- activations: bfloat16 [32, 4, 256, 5120], P('client', None, None, 'row'), may hold values from -6 to 6
- cotangent: bfloat16 [32, 4, 256, 27648], P('client', None, None, 'row'), may hold values from -6 to 6
- lengths: int32 [32, 4], P('client'), may hold values from 1 to 256, 768 in all within a row
- adapter_down: bfloat16 [32, 32, 5120], P('client', None, 'row'), may hold values from -6 to 6
- adapter_up: bfloat16 [32, 32, 27648], P('client', None, 'row'), may hold values from -6 to 6
Outputs:
- merged_down: bfloat16 [32, 5120], P(None, 'row')
- merged_up: bfloat16 [32, 27648], P(None, 'row')
Inputs may be any that keep to these rules, and one draw needn't show every extreme that they name: For each client, its 4 lengths sum to 768, and one of them equals 256; the total holds for one client's row of lengths, not across clients.
All inputs are finite; a program needn't handle non-finite values.
Results may differ from a plain program's by a relative error of at most 0.0046.
Values may be sent and summed in bfloat16 or wider, within the bound.
A program may use at most 64 MiB of HBM per device.

v0:
```python
import jax
import jax.numpy as jnp
from jax import lax
from jax.sharding import PartitionSpec as P

EPS = 1e-06


def local(activations, cotangent, lengths, adapter_down, adapter_up):
    seqs = activations.shape[1]
    span = activations.shape[2]
    inputs = activations[0]
    outputs = cotangent[0]
    down_local = adapter_down[0]
    up_local = adapter_up[0]
    part_in = jnp.dot(
        inputs.reshape(seqs * span, -1), down_local.T, preferred_element_type=jnp.float32
    )
    part_out = jnp.dot(
        outputs.reshape(seqs * span, -1), up_local.T, preferred_element_type=jnp.float32
    )
    projected, pulled = lax.psum((part_in, part_out), "row")
    positions = jnp.arange(span, dtype=jnp.int32)
    seq_lens = lengths[0]
    valid = (positions[None, :] < seq_lens[:, None]).astype(jnp.float32)
    weights = valid / seq_lens.astype(jnp.float32)[:, None]
    proj_w = (projected.reshape(seqs, span, -1) * weights[:, :, None]).astype(jnp.bfloat16)
    pull_w = (pulled.reshape(seqs, span, -1) * weights[:, :, None]).astype(jnp.bfloat16)
    dims = (((1,), (1,)), ((0,), (0,)))
    grad_up = lax.dot_general(proj_w, outputs, dims, preferred_element_type=jnp.float32)
    grad_down = lax.dot_general(pull_w, inputs, dims, preferred_element_type=jnp.float32)
    fisher_up = jnp.sum(grad_up * grad_up, axis=0)
    fisher_down = jnp.sum(grad_down * grad_down, axis=0)
    weighted_down = fisher_down * down_local.astype(jnp.float32)
    weighted_up = fisher_up * up_local.astype(jnp.float32)
    total_wd, total_fd, total_wu, total_fu = lax.psum(
        (weighted_down, fisher_down, weighted_up, fisher_up), "client"
    )
    merged_down = (total_wd / (total_fd + EPS)).astype(jnp.bfloat16)
    merged_up = (total_wu / (total_fu + EPS)).astype(jnp.bfloat16)
    return (merged_down, merged_up)


def solution(mesh):
    in_specs = (
        P("client", None, None, "row"),
        P("client", None, None, "row"),
        P("client", None),
        P("client", None, "row"),
        P("client", None, "row"),
    )
    out_specs = (P(None, "row"), P(None, "row"))
    return jax.shard_map(local, mesh=mesh, in_specs=in_specs, out_specs=out_specs, check_vma=False)
```

profile of v0, /device:TPU:8, one launch (start us, length us, event | category | flops | bytes accessed | tf_op | source)
XLA Modules:
  0.0 419.0 jit_solution(16107752335798554147)
XLA Ops:
  7.2 0.0 copy-start
  7.2 0.0 all-reduce.7.cloned.1.call-start
  7.2 0.0 copy-start.4
  7.2 5.2 %fusion.16 = f32[1024,32]{0,1:T(8,128)S(1)} fusion(bf16[1024,3456]{1,0:T(8,128)(2,1)} %bitcast.35, bf16[1,32,3456]{2,1,0:T(8,128)(2,1)} %param.9), kind=kOutput, calls=%fused_computation.10 | convolution fusion | flops 226492416 | bytes 7430144 | tf_op jit(solution)/shard_map/dot_general | solution.py:19
  12.5 0.0 copy-done
  12.5 0.0 copy-start.6
  12.5 0.0 copy-done.4
  12.5 0.5 fusion.20
  13.0 0.7 copy_bitcast_fusion
  13.7 0.0 all-reduce.7.cloned.1.call-update
  13.8 0.0 all-reduce.5.cloned.1.call-start
  13.8 0.0 copy-done.6
  13.8 0.1 convert_divide_fusion
  13.9 75.9 %all-reduce.7.cloned.1.call-done = (f32[4,256,32]{1,2,0:T(8,128)}, f32[4,256,32]{1,2,0:T(8,128)}) async-done(((f32[4,256,32]{1,2,0:T(8,128)}, f32[4,256,32]{1,2,0:T(8,128)}), (f32[4,256,32]{1,2,0:T(8,128)}, f32[4,256,32]{1,2,0:T(8,128)})) %all-reduce.7.cloned.1.call-update) | async-done | bytes 262160 | tf_op jit(solution)/shard_map/psum | solution.py:22
  89.8 0.0 copy-start.5
  89.8 1.3 fusion.13
  91.1 0.0 copy-start.3
  91.1 0.7 convert_multiply_fusion.1
  91.7 0.0 copy-done.5
  91.7 0.0 copy-start.2
  91.7 4.3 %fusion.5 = f32[32,3456]{1,0:T(8,128)S(1)} fusion(bf16[1,4,256,3456]{3,2,1,0:T(8,128)(2,1)} %param.6, f32[4,256,32]{1,2,0:T(8,128)S(1)} %copy-done.5, f32[4,256]{1,0:T(4,128)S(1)} %convert_divide_fusion), kind=kOutput, calls=%fused_computation.3 | convolution fusion | flops 227332096 | bytes 7655424 | tf_op jit(solution)/shard_map/dot_general | solution.py:30
  96.0 0.0 copy-done.3
  96.0 0.0 copy-done.2
  96.0 0.0 copy-start.1
  96.0 0.9 convert_multiply_fusion
  96.9 0.0 copy-done.1
  97.0 0.0 all-reduce.5.cloned.1.call-update
  97.0 311.7 %all-reduce.5.cloned.1.call-done = (f32[32,640]{1,0:T(8,128)}, f32[32,640]{1,0:T(8,128)}, f32[32,3456]{1,0:T(8,128)}, f32[32,3456]{1,0:T(8,128)}) async-done(((f32[32,640]{1,0:T(8,128)}, f32[32,640]{1,0:T(8,128)}, f32[32,3456]{1,0:T(8,128)}, f32[32,3456]{1,0:T(8,128)}), (f32[32,640]{1,0:T(8,128)}, f32[32,640]{1,0:T(8,128)}, f32[32,3456]{1,0:T(8,128)}, f32[32,3456]{1,0:T(8,128)})) %all-reduce.5.cloned.1.call-update) | async-done | bytes 1048592 | tf_op jit(solution)/shard_map/psum | solution.py:36
  408.7 1.6 divide_convert_fusion.1
  410.3 1.9 divide_convert_fusion
  (1 shorter events, 0.0 us)
Async XLA Ops:
  7.2 5.3 %copy-start = (bf16[1,4,256,640]{3,2,1,0:T(8,128)(2,1)S(1)}, bf16[1,4,256,640]{3,2,1,0:T(8,128)(2,1)}, u32[]{:S(2)}) copy-start(bf16[1,4,256,640]{3,2,1,0:T(8,128)(2,1)} %param.5) | copy-start | bytes 3932164
  7.2 82.6 %all-reduce.7.cloned.1.call-start = ((), (), s32[]{:S(2)}) async-start(), calls=%async_computation.1 | async-start | bytes 524288 | tf_op jit(solution)/shard_map/psum | solution.py:22
  7.2 5.3 %copy-start.4 = (bf16[1,32,640]{2,1,0:T(8,128)(2,1)S(1)}, bf16[1,32,640]{2,1,0:T(8,128)(2,1)}, u32[]{:S(2)}) copy-start(bf16[1,32,640]{2,1,0:T(8,128)(2,1)} %param.8) | copy-start | bytes 122884
  12.5 1.3 copy-start.6
  13.8 394.9 %all-reduce.5.cloned.1.call-start = ((), (), s32[]{:S(2)}) async-start(), calls=%async_computation | async-start | bytes 2097152 | tf_op jit(solution)/shard_map/psum | solution.py:36
  89.8 1.9 copy-start.5
  91.1 4.9 %copy-start.3 = (f32[32,640]{1,0:T(8,128)}, f32[32,640]{1,0:T(8,128)S(1)}, u32[]{:S(2)}) copy-start(f32[32,640]{1,0:T(8,128)S(1)} %fusion.13) | copy-start | bytes 245764
  91.7 4.3 %copy-start.2 = (bf16[1,32,3456]{2,1,0:T(8,128)(2,1)S(1)}, bf16[1,32,3456]{2,1,0:T(8,128)(2,1)}, u32[]{:S(2)}) copy-start(bf16[1,32,3456]{2,1,0:T(8,128)(2,1)} %param.9) | copy-start | bytes 663556
  96.0 0.9 copy-start.1
Sparse Core Ops, SparseCore 0:
  13.9 75.8 all-reduce.6
  97.1 311.5 all-reduce.4
where the time goes:
time: 419 us
  waiting for transfers between devices  388 us (93%)
  between operations  14.1 us (3%)
  matrix products  11.2 us (3%)
  other arithmetic  5.09 us (1%)
    psum x1, waiting for transfers between devices, local(): lax.psum((weighted_down, fisher_down, weighted_up, fisher_up), 'client')  312 us
    psum x1, waiting for transfers between devices, local(): projected, pulled = lax.psum((part_in, part_out), 'row')  75.9 us
  transfers between devices with their start and end apart: 2, of which 2 were waited for; matrix products, arithmetic and copies ran while one was open for 0% of the time, Pallas kernels for 0%

commit v1 on v0

v1 whole, which is shorter than its diff:
```python
import functools

import jax
import jax.numpy as jnp
from jax import lax
from jax.experimental import pallas as pl
from jax.experimental.pallas import tpu as pltpu
from jax.sharding import PartitionSpec as P

EPS = 1e-06
MESH = pl.DeviceIdType.MESH
LANES = 128
F32 = jnp.float32
BF16 = jnp.bfloat16
PART = F32
NT = (((1,), (1,)), ((), ()))


def kernel(
    nc, nr, act, cot, lens, down, up, out,
    data, adapt, lens_s, part, arrived, mine, tokens, terms, received, merged, gathered,
    load_sem, small_sem, rs_send, rs_recv, ag_send, ag_recv, cl_send, cl_recv, out_send, out_recv, copy_sem,
):
    seqs, span, wa = act.shape[1:]
    wc = cot.shape[3]
    rank = down.shape[1]
    c = lax.axis_index("client")
    r = lax.axis_index("row")

    barrier = pltpu.get_barrier_semaphore()

    def greet_row(k, _):
        pl.semaphore_signal(barrier, inc=1, device_id=(c, lax.rem(r + k, nr)), device_id_type=MESH)
        return 0

    def greet_client(k, _):
        pl.semaphore_signal(barrier, inc=1, device_id=(lax.rem(c + k, nc), r), device_id_type=MESH)
        return 0

    lax.fori_loop(1, nr, greet_row, 0)
    lax.fori_loop(1, nc, greet_client, 0)

    small = [
        pltpu.make_async_copy(up.at[0], adapt.at[:, pl.ds(0, wc)], small_sem.at[0]),
        pltpu.make_async_copy(down.at[0], adapt.at[:, pl.ds(wc, wa)], small_sem.at[1]),
        pltpu.make_async_copy(lens, lens_s, small_sem.at[2]),
    ]
    for copy in small:
        copy.start()
    loads = []
    for e in range(seqs):
        loads.append((
            pltpu.make_async_copy(cot.at[0, e], data.at[e, :, pl.ds(0, wc)], load_sem.at[2 * e]),
            pltpu.make_async_copy(act.at[0, e], data.at[e, :, pl.ds(wc, wa)], load_sem.at[2 * e + 1]),
        ))
        for copy in loads[e]:
            copy.start()
    for copy in small:
        copy.wait()

    half = span // 2
    rows = 2 * rank // 4

    def scatter(e, k):
        to = lax.rem(r + k, nr)
        return pltpu.make_async_remote_copy(
            src_ref=part.at[e, to], dst_ref=arrived.at[e, k - 1],
            send_sem=rs_send.at[e], recv_sem=rs_recv.at[e],
            device_id=(c, to), device_id_type=MESH,
        )

    def spread(e, k):
        to = lax.rem(r + k, nr)
        return pltpu.make_async_remote_copy(
            src_ref=mine.at[e], dst_ref=tokens.at[e, r],
            send_sem=ag_send.at[e], recv_sem=ag_recv.at[e],
            device_id=(c, to), device_id_type=MESH,
        )

    for e in range(seqs):
        with jax.named_scope("project"):
            for copy in loads[e]:
                copy.wait()
            pulled = lax.dot_general(adapt[:, :wc], data[e, :, :wc], NT, preferred_element_type=F32)
            projected = lax.dot_general(adapt[:, wc:], data[e, :, wc:], NT, preferred_element_type=F32)
            for b in range(nr):
                source = projected if b < nr // 2 else pulled
                top, left = (b // 2) % 2 * rows, b % 2 * half
                part[e, b] = source[top:top + rows, left:left + half].astype(PART)
        if e == 0:
            with jax.named_scope("barrier"):
                pl.semaphore_wait(barrier, nr - 1 + nc - 1)
        for k in range(1, nr):
            scatter(e, k).start()

    position = lax.broadcasted_iota(jnp.int32, (1, half), 1) + lax.rem(r, 2) * half
    for e in range(seqs):
        with jax.named_scope("rowsum"):
            pltpu.make_async_remote_copy(
                src_ref=part.at[e, pl.ds(0, nr - 1)], dst_ref=arrived.at[e],
                send_sem=rs_send.at[e], recv_sem=rs_recv.at[e], device_id=(c, r), device_id_type=MESH,
            ).wait()
            total = part[e, r].astype(F32)
            for k in range(nr - 1):
                total += arrived[e, k].astype(F32)
            length = jnp.full((1, half), lens_s[0, e], jnp.int32)
            weight = (position < length).astype(F32) / length.astype(F32)
            mine[e] = (total * weight).astype(BF16)
            tokens[e, r] = mine[e]
        for k in range(1, nr):
            spread(e, k).start()

    for e in range(seqs):
        with jax.named_scope("rowgather"):
            pltpu.make_async_remote_copy(
                src_ref=tokens.at[e, pl.ds(0, nr - 1)], dst_ref=tokens.at[e, pl.ds(0, nr - 1)],
                send_sem=ag_send.at[e], recv_sem=ag_recv.at[e], device_id=(c, r), device_id_type=MESH,
            ).wait()

    def fishers(block):
        columns = pl.ds(pl.multiple_of(block * LANES, LANES), LANES)
        first = (block < wc // LANES).astype(jnp.int32)
        base = (1 - first) * (nr // 2)
        total = jnp.zeros((rank, LANES), F32)
        for e in range(seqs):
            lines = [
                jnp.concatenate([tokens[e, base + 2 * i], tokens[e, base + 2 * i + 1]], axis=1)
                for i in range(nr // 4)
            ]
            grad = jnp.dot(jnp.concatenate(lines, axis=0), data[e, :, columns], preferred_element_type=F32)
            total += grad * grad
        return total * adapt[:, columns].astype(F32), total

    def give(block, slot):
        return pltpu.make_async_remote_copy(
            src_ref=terms.at[slot], dst_ref=received.at[slot],
            send_sem=cl_send, recv_sem=cl_recv,
            device_id=(block, r), device_id_type=MESH,
        )

    def column(k, _):
        block = lax.rem(c + k, nc)
        weighted, fisher = fishers(block)
        terms[k - 1, :rank] = weighted.astype(BF16)
        terms[k - 1, rank:] = fisher.astype(BF16)
        give(block, k - 1).start()
        return 0

    with jax.named_scope("grads"):
        lax.fori_loop(1, nc, column, 0)
        weighted, fisher = fishers(c)

    with jax.named_scope("clientsum"):
        give(c, pl.ds(0, nc - 1)).wait()
        for k in range(nc - 1):
            weighted += received[k, :rank].astype(F32)
            fisher += received[k, rank:].astype(F32)
        merged[...] = (weighted / (fisher + EPS)).astype(BF16)

    def publish(k, _):
        pltpu.make_async_remote_copy(
            src_ref=merged, dst_ref=gathered.at[c],
            send_sem=out_send, recv_sem=out_recv,
            device_id=(lax.rem(c + k, nc), r), device_id_type=MESH,
        ).start()
        return 0

    lax.fori_loop(1, nc, publish, 0)
    gathered[c] = merged[...]
    with jax.named_scope("clientgather"):
        pltpu.make_async_remote_copy(
            src_ref=gathered.at[pl.ds(0, nc - 1)], dst_ref=gathered.at[pl.ds(0, nc - 1)],
            send_sem=out_send, recv_sem=out_recv, device_id=(c, r), device_id_type=MESH,
        ).wait()
    with jax.named_scope("writeout"):
        for b in range(nc):
            out[:, b * LANES:(b + 1) * LANES] = gathered[b]


def local(nc, nr, activations, cotangent, lengths, adapter_down, adapter_up):
    _, seqs, span, wa = activations.shape
    wc = cotangent.shape[3]
    rank = adapter_down.shape[1]
    width = wa + wc
    rows, half = 2 * rank // 4, span // 2
    hbm = pl.BlockSpec(memory_space=pl.ANY)
    out = pl.pallas_call(
        functools.partial(kernel, nc, nr),
        out_shape=jax.ShapeDtypeStruct((rank, width), BF16),
        in_specs=[hbm] * 5,
        out_specs=pl.BlockSpec(memory_space=pltpu.VMEM),
        scratch_shapes=[
            pltpu.VMEM((seqs, span, width), BF16),
            pltpu.VMEM((rank, width), BF16),
            pltpu.SMEM((1, seqs), jnp.int32),
            pltpu.VMEM((seqs, nr, rows, half), PART),
            pltpu.VMEM((seqs, nr - 1, rows, half), PART),
            pltpu.VMEM((seqs, rows, half), BF16),
            pltpu.VMEM((seqs, nr, rows, half), BF16),
            pltpu.VMEM((nc - 1, 2 * rank, LANES), BF16),
            pltpu.VMEM((nc - 1, 2 * rank, LANES), BF16),
            pltpu.VMEM((rank, LANES), BF16),
            pltpu.VMEM((nc, rank, LANES), BF16),
            pltpu.SemaphoreType.DMA((2 * seqs,)),
            pltpu.SemaphoreType.DMA((3,)),
            pltpu.SemaphoreType.DMA((seqs,)),
            pltpu.SemaphoreType.DMA((seqs,)),
            pltpu.SemaphoreType.DMA((seqs,)),
            pltpu.SemaphoreType.DMA((seqs,)),
            pltpu.SemaphoreType.DMA,
            pltpu.SemaphoreType.DMA,
            pltpu.SemaphoreType.DMA,
            pltpu.SemaphoreType.DMA,
            pltpu.SemaphoreType.DMA,
        ],
        compiler_params=pltpu.CompilerParams(
            collective_id=0, has_side_effects=True, vmem_limit_bytes=48 * 1024 * 1024
        ),
    )(activations, cotangent, lengths, adapter_down, adapter_up)
    return out[:, wc:], out[:, :wc]


def solution(mesh):
    in_specs = (
        P("client", None, None, "row"),
        P("client", None, None, "row"),
        P("client", None),
        P("client", None, "row"),
        P("client", None, "row"),
    )
    out_specs = (P(None, "row"), P(None, "row"))
    body = functools.partial(local, mesh.shape["client"], mesh.shape["row"])
    return jax.shard_map(body, mesh=mesh, in_specs=in_specs, out_specs=out_specs, check_vma=False)
```

time: 419 us -> 47.4 us (0.11)
  the two profiles are of different devices: /device:TPU:8 before, /device:TPU:1 now
where the time goes in v1:
time: 47.4 us; the launch traced here: 47.1 us
  Pallas kernels  41.5 us (88%)
  local copies, waits for them, and re-layouts  5 us (11%)
  between operations  0.65 us (1%)
    pallas_call x1, Pallas kernels, local(): pl.pallas_call(functools.partial(kernel, nc, nr), out_shape=jax.ShapeDtyp...  41.5 us
    unnamed x8, local copies, waits for them, and re-layouts  3.68 us
    slice x2, local copies, waits for them, and re-layouts, local(): return (out[:, wc:], out[:, :wc])  1.32 us

profile of v1, /device:TPU:1, one launch (start us, length us, event | category | flops | bytes accessed | tf_op | source)
XLA Modules:
  0.0 47.1 jit_solution(13432661522610002601)
XLA Ops:
  0.6 0.0 copy-start
  0.6 1.3 %copy-done = bf16[1,4,256,640]{3,2,1,0:T(8,128)(2,1)S(1)} copy-done((bf16[1,4,256,640]{3,2,1,0:T(8,128)(2,1)S(1)}, bf16[1,4,256,640]{3,2,1,0:T(8,128)(2,1)}, u32[]{:S(2)}) %copy-start) | copy-done | bytes 1310744
  1.9 0.0 copy-start.1
  2.0 0.9 %copy-done.1 = bf16[1,32,3456]{2,1,0:T(8,128)(2,1)S(1)} copy-done((bf16[1,32,3456]{2,1,0:T(8,128)(2,1)S(1)}, bf16[1,32,3456]{2,1,0:T(8,128)(2,1)}, u32[]{:S(2)}) %copy-start.1) | copy-done | bytes 221208
  2.9 0.0 copy-start.2
  2.9 0.8 %copy-done.2 = bf16[1,32,640]{2,1,0:T(8,128)(2,1)S(1)} copy-done((bf16[1,32,640]{2,1,0:T(8,128)(2,1)S(1)}, bf16[1,32,640]{2,1,0:T(8,128)(2,1)}, u32[]{:S(2)}) %copy-start.2) | copy-done | bytes 40984
  3.7 0.0 copy-start.3
  3.7 0.7 %copy-done.3 = s32[1,4]{1,0:T(1,128)S(1)} copy-done((s32[1,4]{1,0:T(1,128)S(1)}, s32[1,4]{1,0:T(1,128)}, u32[]{:S(2)}) %copy-start.3) | copy-done | bytes 40
  4.3 41.5 %shard_map.68 = bf16[32,4096]{1,0:T(8,128)(2,1)S(1)} custom-call(bf16[1,4,256,640]{3,2,1,0:T(8,128)(2,1)S(1)} %copy-done, bf16[1,4,256,3456]{3,2,1,0:T(8,128)(2,1)} %cot.1, s32[1,4]{1,0:T(1,128)S(1)} %copy-done.3, bf16[1,32,640]{2,1,0:T(8,128)(2,1)S(1)} %copy-done.2, bf16[1,32,3456]{2,1,0:T(8,128)(2,1)S(1)} %copy-done.1), custom_call_target="tpu_custom_call" | custom-call | tf_op jit(solution)/shard_map/pallas_call | solution.py:187
  45.8 0.6 %slice.6 = bf16[32,640]{1,0:T(8,128)(2,1)} slice(bf16[32,4096]{1,0:T(8,128)(2,1)S(1)} %shard_map.68), slice={[0:32], [3456:4096]} | slice | bytes 81920 | tf_op jit(solution)/shard_map/slice | solution.py:220
  46.4 0.7 %slice.7 = bf16[32,3456]{1,0:T(8,128)(2,1)} slice(bf16[32,4096]{1,0:T(8,128)(2,1)S(1)} %shard_map.68), slice={[0:32], [0:3456]} | slice | bytes 442368 | tf_op jit(solution)/shard_map/slice | solution.py:220
Async XLA Ops:
  0.6 1.3 %copy-start = (bf16[1,4,256,640]{3,2,1,0:T(8,128)(2,1)S(1)}, bf16[1,4,256,640]{3,2,1,0:T(8,128)(2,1)}, u32[]{:S(2)}) copy-start(bf16[1,4,256,640]{3,2,1,0:T(8,128)(2,1)} %act.1) | copy-start | bytes 3932164
  1.9 0.9 %copy-start.1 = (bf16[1,32,3456]{2,1,0:T(8,128)(2,1)S(1)}, bf16[1,32,3456]{2,1,0:T(8,128)(2,1)}, u32[]{:S(2)}) copy-start(bf16[1,32,3456]{2,1,0:T(8,128)(2,1)} %up.1) | copy-start | bytes 663556
  2.9 0.8 %copy-start.2 = (bf16[1,32,640]{2,1,0:T(8,128)(2,1)S(1)}, bf16[1,32,640]{2,1,0:T(8,128)(2,1)}, u32[]{:S(2)}) copy-start(bf16[1,32,640]{2,1,0:T(8,128)(2,1)} %down.1) | copy-start | bytes 122884
  3.7 0.7 %copy-start.3 = (s32[1,4]{1,0:T(1,128)S(1)}, s32[1,4]{1,0:T(1,128)}, u32[]{:S(2)}) copy-start(s32[1,4]{1,0:T(1,128)} %lens.1) | copy-start | bytes 52

commit v2 on v0

v2 whole, which is shorter than its diff:
```python
import functools

import jax
import jax.numpy as jnp
from jax import lax
from jax.experimental import pallas as pl
from jax.experimental.pallas import tpu as pltpu
from jax.sharding import PartitionSpec as P

EPS = 1e-06
MESH = pl.DeviceIdType.MESH
LANES = 128
F32 = jnp.float32
BF16 = jnp.bfloat16
NT = (((1,), (1,)), ((), ()))
NX, NL, NY = 4, 2, 4
NH, NCORE = 4, 2
PLANE = NL * NY
UP_BLOCKS = 27
SPAN = 7
PROJECTED, PULLED = 0, 1
FINISH_AT = 2


def hops(offset):
    dx, dl, dy = offset
    return min(dx, NX - dx) + dl + min(dy, NY - dy)


def kernel(
    act, cot, lens, down, up, out,
    data, adapt, lens_s, part, sibling, pair, arrived, tokens, terms, dterms, received, own, merged, gathered,
    load_sem, small_sem, ex_send, ex_recv, bc_send, bc_recv, tk_send, tk_recv,
    up_send, up_recv, dn_send, dn_recv, out_send, out_recv,
):
    seqs, span, wa = act.shape[1:]
    wc = cot.shape[3]
    rank = down.shape[1]
    half = rank // 2
    c = lax.axis_index("client")
    r = lax.axis_index("row")
    x, lo, y = c // PLANE, (c // NY) % NL, c % NY
    hi, core = r // NCORE, r % NCORE

    def client(offset):
        dx, dl, dy = offset
        return lax.rem(x + dx, NX) * PLANE + lax.rem(lo + dl, NL) * NY + lax.rem(y + dy, NY)

    def chip(k):
        return lax.rem(hi + k, NH) * NCORE + core

    offsets = [(dx, dl, dy) for dx in range(NX) for dl in range(NL) for dy in range(NY)]
    offsets = sorted(offsets, key=lambda o: -hops(o))[:-1]
    peers = [(c, hi * NCORE + 1 - core)] + [(c, chip(k)) for k in (2, 1, 3)]
    peers += [(client(o), r) for o in offsets]
    other = peers[0]

    small = [
        pltpu.make_async_copy(down.at[0], adapt.at[:, pl.ds(wc, wa)], small_sem.at[0]),
        pltpu.make_async_copy(up.at[0], adapt.at[:, pl.ds(0, wc)], small_sem.at[1]),
        pltpu.make_async_copy(lens, lens_s, small_sem.at[2]),
    ]
    load_act = pltpu.make_async_copy(act.at[0], data.at[:, :, pl.ds(wc, wa)], load_sem.at[seqs])
    load_cot = [
        pltpu.make_async_copy(cot.at[0, e], data.at[e, :, pl.ds(0, wc)], load_sem.at[e])
        for e in range(seqs)
    ]
    for copy in [small[0], load_act, small[1]] + load_cot + [small[2]]:
        copy.start()

    barrier = pltpu.get_barrier_semaphore()
    for peer in peers:
        pl.semaphore_signal(barrier, inc=1, device_id=peer, device_id_type=MESH)

    def remote(src, dst, send, recv, to):
        return pltpu.make_async_remote_copy(
            src_ref=src, dst_ref=dst, send_sem=send, recv_sem=recv, device_id=to, device_id_type=MESH
        )

    def exchange(step):
        if step == 0:
            return remote(part.at[PROJECTED, 1 - core], sibling.at[PROJECTED], ex_send.at[0], ex_recv.at[0], other)
        e = step - 1
        return remote(part.at[PULLED, 1 - core, e], sibling.at[PULLED, e], ex_send.at[step], ex_recv.at[step], other)

    def broadcast(step):
        exchange(step).wait_recv()
        if step == 0:
            pair[PROJECTED] = (part[PROJECTED, core] + sibling[PROJECTED]).astype(BF16)
        else:
            e = step - 1
            pair[PULLED, e] = (part[PULLED, core, e] + sibling[PULLED, e]).astype(BF16)
        for k in (2, 1, 3):
            if step == 0:
                src, dst = pair.at[PROJECTED], arrived.at[PROJECTED, k - 1]
            else:
                src, dst = pair.at[PULLED, e], arrived.at[PULLED, k - 1, e]
            remote(src, dst, bc_send.at[step], bc_recv.at[step], (c, chip(k))).start()

    def broadcast_all(step):
        if step == 0:
            ref = arrived.at[PROJECTED]
        else:
            ref = arrived.at[PULLED, :, step - 1]
        return remote(ref, ref, bc_send.at[step], bc_recv.at[step], other)

    def token_swap(kind):
        ref = tokens.at[kind, core]
        return remote(ref, ref, tk_send.at[kind], tk_recv.at[kind], other)

    def finish(kind):
        for step in ((0,) if kind == PROJECTED else range(1, 1 + seqs)):
            broadcast_all(step).wait_recv()
        position = lax.broadcasted_iota(jnp.int32, (1, span), 1)
        for e in range(seqs):
            total = part[kind, core, e] + sibling[kind, e]
            for k in range(NH - 1):
                total += arrived[kind, k, e].astype(F32)
            length = jnp.full((1, span), lens_s[0, e], jnp.int32)
            weight = (position < length).astype(F32) / length.astype(F32)
            tokens[kind, core, e] = (total * weight).astype(BF16)
        token_swap(kind).start()

    load_act.wait()
    small[0].wait()
    for e in range(seqs):
        projected = lax.dot_general(adapt[:, wc:], data[e, :, wc:], NT, preferred_element_type=F32)
        part[PROJECTED, 0, e] = projected[:half]
        part[PROJECTED, 1, e] = projected[half:]
    pl.semaphore_wait(barrier, len(peers))
    exchange(0).start()
    small[1].wait()
    for e in range(seqs):
        load_cot[e].wait()
        pulled = lax.dot_general(adapt[:, :wc], data[e, :, :wc], NT, preferred_element_type=F32)
        part[PULLED, 0, e] = pulled[:half]
        part[PULLED, 1, e] = pulled[half:]
        exchange(1 + e).start()
        broadcast(e)
    broadcast(seqs)
    small[2].wait()
    finish(PROJECTED)

    def fishers(kind, columns, width):
        total = jnp.zeros((rank, width), F32)
        for e in range(seqs):
            left = jnp.concatenate([tokens[kind, 0, e], tokens[kind, 1, e]], axis=0)
            grad = jnp.dot(left, data[e, :, columns], preferred_element_type=F32)
            total += grad * grad
        return (total * adapt[:, columns].astype(F32)).astype(BF16), total.astype(BF16)

    def units(weighted, fisher, b):
        columns = slice(b * LANES, (b + 1) * LANES)
        return [
            jnp.concatenate([weighted[h * half:(h + 1) * half, columns], fisher[h * half:(h + 1) * half, columns]], axis=0)
            for h in range(2)
        ]

    def is_whole(p, j):
        return j < jnp.where(p < NX - 1, 6, 4)

    def up_index(p, j):
        return jnp.where(p < NX - 1, jnp.minimum(j, SPAN - 1), jnp.where(j < 4, j + 1, 5 + (j - 4) // 2))

    def give_up(stage, offset):
        to = client(offset)
        p, j = to // PLANE, to % PLANE
        index = up_index(p, j)
        slot = offset[0] * PLANE + offset[1] * NY + offset[2] - 1

        @pl.when(is_whole(p, j))
        def _():
            remote(terms.at[stage, index], received.at[pl.ds(2 * slot, 2)], up_send, up_recv, (to, r)).start()

        @pl.when(jnp.logical_not(is_whole(p, j)))
        def _():
            remote(terms.at[stage, index, j % 2], received.at[2 * slot], up_send, up_recv, (to, r)).start()

    token_swap(PROJECTED).wait_recv()
    steps = (2, 1, 3, 0)

    def up_stage(stage):
        dx = steps[stage]
        p = lax.rem(x + dx, NX)
        first = jnp.minimum(p * SPAN, UP_BLOCKS - SPAN)
        columns = pl.ds(pl.multiple_of(first * LANES, LANES), SPAN * LANES)
        weighted, fisher = fishers(PROJECTED, columns, SPAN * LANES)
        for b in range(SPAN):
            for h, unit in enumerate(units(weighted, fisher, b)):
                terms[stage, b, h] = unit
        for offset in offsets:
            if offset[0] == dx:
                give_up(stage, offset)

    for stage in range(NX):
        if stage == FINISH_AT:
            finish(PULLED)
        up_stage(stage)

    token_swap(PULLED).wait_recv()
    weighted, fisher = fishers(PULLED, pl.ds(wc, wa), wa)
    for b in range(wa // LANES):
        for h, unit in enumerate(units(weighted, fisher, b)):
            dterms[2 * b + h] = unit
    down_units = 2 * (wa // LANES)
    for k in range(down_units):
        n = lax.rem(c + k, down_units)
        to = jnp.minimum(n // 2, NX - 1) * PLANE + jnp.where(n < 6, 6 + n % 2, n - 2)
        dx, dl, dy = lax.rem(to // PLANE - x + NX, NX), lax.rem(to // NY % NL - lo + NL, NL), lax.rem(to % NY - y + NY, NY)
        slot = dx * PLANE + dl * NY + dy - 1

        @pl.when(c != to)
        def _():
            remote(dterms.at[n], received.at[2 * slot + 1], dn_send, dn_recv, (to, r)).start()

    j = c % PLANE
    whole = is_whole(x, j)
    split = jnp.logical_not(whole)
    peers_n = NX * PLANE - 1
    mine = terms.at[NX - 1, up_index(x, j)]

    @pl.when(whole)
    def _():
        remote(received, received, up_send, up_recv, other).wait_recv()
        own[...] = mine[...]

    @pl.when(split)
    def _():
        ref = received.at[pl.ds(0, peers_n)]
        remote(ref, ref, up_send, up_recv, other).wait_recv()
        remote(ref, ref, dn_send, dn_recv, other).wait_recv()
        own[0] = mine[j % 2]
        own[1] = dterms[jnp.where(x < NX - 1, 2 * x + j % 2, j + 2)]

    for u in range(2):
        total = own[u].astype(F32)
        for slot in range(peers_n):
            total += received[2 * slot + u].astype(F32)
        merged[u] = (total[:half] / (total[half:] + EPS)).astype(BF16)
    for offset in offsets:
        remote(merged, gathered.at[c], out_send, out_recv, (client(offset), r)).start()
    gathered[c] = merged[...]

    for step in range(1 + seqs):
        exchange(step).wait_send()
        broadcast_all(step).wait_send()
    for kind in (PROJECTED, PULLED):
        token_swap(kind).wait_send()

    def sent(n, sem):
        ref = received.at[pl.ds(0, n)]
        remote(ref, ref, sem, sem, other).wait_send()

    @pl.when(whole)
    def _():
        sent(2 * 21 + 10, up_send)
        sent(10, dn_send)

    @pl.when(split)
    def _():
        sent(2 * 22 + 9, up_send)
        sent(9, dn_send)

    ref = gathered.at[pl.ds(0, peers_n)]
    remote(ref, ref, out_send, out_recv, other).wait()
    for owner in range(NX * PLANE):
        p, j = owner // PLANE, owner % PLANE
        if j < (6 if p < NX - 1 else 4):
            block = SPAN * p + j
            for h in range(2):
                out[h * half:(h + 1) * half, block * LANES:(block + 1) * LANES] = gathered[owner, h]
        else:
            block, dblock = (SPAN * p + 6, p) if p < NX - 1 else (25 + (j - 4) // 2, 3 + (j - 4) // 2)
            h = j % 2
            out[h * half:(h + 1) * half, block * LANES:(block + 1) * LANES] = gathered[owner, 0]
            out[h * half:(h + 1) * half, wc + dblock * LANES:wc + (dblock + 1) * LANES] = gathered[owner, 1]


def local(activations, cotangent, lengths, adapter_down, adapter_up):
    _, seqs, span, wa = activations.shape
    wc = cotangent.shape[3]
    rank = adapter_down.shape[1]
    half = rank // 2
    width = wa + wc
    owners = NX * PLANE
    hbm = pl.BlockSpec(memory_space=pl.ANY)
    dma = pltpu.SemaphoreType.DMA
    out = pl.pallas_call(
        kernel,
        out_shape=jax.ShapeDtypeStruct((rank, width), BF16),
        in_specs=[hbm] * 5,
        out_specs=pl.BlockSpec(memory_space=pltpu.VMEM),
        scratch_shapes=[
            pltpu.VMEM((seqs, span, width), BF16),
            pltpu.VMEM((rank, width), BF16),
            pltpu.SMEM((1, seqs), jnp.int32),
            pltpu.VMEM((2, 2, seqs, half, span), F32),
            pltpu.VMEM((2, seqs, half, span), F32),
            pltpu.VMEM((2, seqs, half, span), BF16),
            pltpu.VMEM((2, NH - 1, seqs, half, span), BF16),
            pltpu.VMEM((2, 2, seqs, half, span), BF16),
            pltpu.VMEM((NX, SPAN, 2, rank, LANES), BF16),
            pltpu.VMEM((2 * (wa // LANES), rank, LANES), BF16),
            pltpu.VMEM((2 * (owners - 1), rank, LANES), BF16),
            pltpu.VMEM((2, rank, LANES), BF16),
            pltpu.VMEM((2, half, LANES), BF16),
            pltpu.VMEM((owners, 2, half, LANES), BF16),
            dma((seqs + 1,)), dma((3,)),
            dma((seqs + 1,)), dma((seqs + 1,)), dma((seqs + 1,)), dma((seqs + 1,)), dma((2,)), dma((2,)),
            dma, dma, dma, dma, dma, dma,
        ],
        compiler_params=pltpu.CompilerParams(
            collective_id=0, has_side_effects=True, vmem_limit_bytes=48 * 1024 * 1024
        ),
    )(*(pltpu.with_memory_space_constraint(a, pltpu.HBM) for a in (activations, cotangent, lengths, adapter_down, adapter_up)))
    return out[:, wc:], out[:, :wc]


def solution(mesh):
    in_specs = (
        P("client", None, None, "row"),
        P("client", None, None, "row"),
        P("client", None),
        P("client", None, "row"),
        P("client", None, "row"),
    )
    out_specs = (P(None, "row"), P(None, "row"))
    return jax.shard_map(local, mesh=mesh, in_specs=in_specs, out_specs=out_specs, check_vma=False)
```

time: 419 us -> 37.3 us (0.09)
  the two profiles are of different devices: /device:TPU:8 before, /device:TPU:1 now
where the time goes in v2:
time: 37.3 us; the launch traced here: 37.2 us
  Pallas kernels  35.3 us (95%)
  local copies, waits for them, and re-layouts  1.32 us (4%)
  between operations  0.64 us (2%)
    pallas_call x1, Pallas kernels, local(): pl.pallas_call(kernel, out_shape=jax.ShapeDtypeStruct((rank, width), BF16...  35.3 us
    slice x2, local copies, waits for them, and re-layouts, local(): return (out[:, wc:], out[:, :wc])  1.32 us

profile of v2, /device:TPU:1, one launch (start us, length us, event | category | flops | bytes accessed | tf_op | source)
XLA Modules:
  0.0 37.2 jit_solution(12911559855597691679)
XLA Ops:
  0.6 35.3 %shard_map.68 = bf16[32,4096]{1,0:T(8,128)(2,1)S(1)} custom-call(bf16[1,4,256,640]{3,2,1,0:T(8,128)(2,1)} %act.1, bf16[1,4,256,3456]{3,2,1,0:T(8,128)(2,1)} %cot.1, s32[1,4]{1,0:T(1,128)} %lens.1, bf16[1,32,640]{2,1,0:T(8,128)(2,1)} %down.1, bf16[1,32,3456]{2,1,0:T(8,128)(2,1)} %up.1), custom_call_target="tpu_custom_call" | custom-call | tf_op jit(solution)/shard_map/pallas_call | solution.py:288
  35.9 0.6 %slice.6 = bf16[32,640]{1,0:T(8,128)(2,1)} slice(bf16[32,4096]{1,0:T(8,128)(2,1)S(1)} %shard_map.68), slice={[0:32], [3456:4096]} | slice | bytes 81920 | tf_op jit(solution)/shard_map/slice | solution.py:316
  36.5 0.7 %slice.7 = bf16[32,3456]{1,0:T(8,128)(2,1)} slice(bf16[32,4096]{1,0:T(8,128)(2,1)S(1)} %shard_map.68), slice={[0:32], [0:3456]} | slice | bytes 442368 | tf_op jit(solution)/shard_map/slice | solution.py:316

commit v3 on v2

v3 whole, which is shorter than its diff:
```python
import jax
import jax.numpy as jnp
from jax import lax
from jax.experimental import pallas as pl
from jax.experimental.pallas import tpu as pltpu
from jax.sharding import PartitionSpec as P

EPS = 1e-06
MESH = pl.DeviceIdType.MESH
LANES = 128
F32 = jnp.float32
BF16 = jnp.bfloat16
NT = (((1,), (1,)), ((), ()))
NX, NL, NY = 4, 2, 4
NH, NCORE = 4, 2
PLANE = NL * NY
OWNERS = NX * PLANE
UP_BLOCKS = 27
SPAN = 7
PROJECTED, PULLED = 0, 1
FINISH_AT = 3


def pick(v, a, b, c, d):
    return jnp.where(v == 0, a, jnp.where(v == 1, b, jnp.where(v == 2, c, d)))


def kernel(
    act, cot, lens, down, up, out,
    data, adapt, lens_s, part, sibling, pair, arrived, tokens, terms, dterms, factors, fishers_in, own, merged, gathered,
    load_sem, small_sem, ex_send, ex_recv, bc_send, bc_recv, tk_send, tk_recv,
    a_send, a_recv, f_send, f_recv, out_send, out_recv, plane_sem, all_sem,
):
    seqs, span, wa = act.shape[1:]
    wc = cot.shape[3]
    rank = down.shape[1]
    half = rank // 2
    mid = seqs // 2
    c = lax.axis_index("client")
    r = lax.axis_index("row")
    x, lo, y = c // PLANE, (c // NY) % NL, c % NY
    hi, core = r // NCORE, r % NCORE

    def client(dx, dl, dy):
        return lax.rem(x + dx, NX) * PLANE + lax.rem(lo + dl, NL) * NY + lax.rem(y + dy, NY)

    def chip(k):
        return (c, lax.rem(hi + k, NH) * NCORE + core)

    def target(k):
        v, q = k // PLANE, k % PLANE
        return client(pick(v, 2, 1, 3, 0), 1 - q // NY, pick(q % NY, 2, 1, 3, 0))

    def slot_at(to):
        dx, dl, dy = lax.rem(to // PLANE - x + NX, NX), lax.rem(to // NY % NL - lo + NL, NL), lax.rem(to % NY - y + NY, NY)
        return pick(dx, 3, 1, 0, 2) * PLANE + (1 - dl) * NY + pick(dy, 3, 1, 0, 2)

    def rows(unit, n):
        return pl.ds(pl.multiple_of(unit * half, half), n * half)

    def lanes(block):
        return pl.ds(pl.multiple_of(block * LANES, LANES), LANES)

    def is_whole(p, j):
        return j < jnp.where(p < NX - 1, 6, 4)

    def up_block(p, j):
        return jnp.where(p < NX - 1, p * SPAN + jnp.minimum(j, SPAN - 1), jnp.where(j < 4, 21 + j, 25 + (j - 4) // 2))

    def down_block(p, j):
        return jnp.where(p < NX - 1, p, 3 + (j - 4) // 2)

    def first_block(p):
        return jnp.minimum(p * SPAN, UP_BLOCKS - SPAN)

    other = (c, hi * NCORE + 1 - core)
    peers = [other] + [chip(k) for k in (2, 1, 3)]
    along_y = [(client(0, 0, k), r) for k in (2, 1, 3)]
    peers += [(client(k, 0, 0), r) for k in (2, 1, 3)] + along_y + [(client(0, 1, 0), r)]

    small = [
        pltpu.make_async_copy(down.at[0], adapt.at[:, pl.ds(wc, wa)], small_sem.at[0]),
        pltpu.make_async_copy(up.at[0], adapt.at[:, pl.ds(0, wc)], small_sem.at[1]),
        pltpu.make_async_copy(lens, lens_s, small_sem.at[2]),
    ]
    load_act = pltpu.make_async_copy(act.at[0], data.at[:, :, pl.ds(wc, wa)], load_sem.at[seqs])

    def load_cot(e):
        return pltpu.make_async_copy(cot.at[0, e], data.at[e, :, pl.ds(0, wc)], load_sem.at[e])

    for copy in [small[0], load_act, small[1]] + [load_cot(e) for e in range(seqs)] + [small[2]]:
        copy.start()

    barrier = pltpu.get_barrier_semaphore()
    for peer in peers:
        pl.semaphore_signal(barrier, inc=1, device_id=peer, device_id_type=MESH)

    def remote(src, dst, send, recv, to):
        return pltpu.make_async_remote_copy(
            src_ref=src, dst_ref=dst, send_sem=send, recv_sem=recv, device_id=to, device_id_type=MESH
        )

    def piece(step):
        return (PROJECTED, pl.ds(0, seqs)) if step == 0 else (PULLED, pl.ds((step - 1) * mid, mid))

    def exchange(step):
        kind, which = piece(step)
        return remote(part.at[kind, 1 - core, which], sibling.at[kind, which], ex_send.at[step], ex_recv.at[step], other)

    def broadcast(step):
        kind, which = piece(step)
        exchange(step).wait_recv()
        pair[kind, which] = (part[kind, core, which] + sibling[kind, which]).astype(BF16)
        for k in (2, 1, 3):
            remote(pair.at[kind, which], arrived.at[kind, k - 1, which], bc_send.at[step], bc_recv.at[step], chip(k)).start()

    def broadcast_all(step):
        kind, which = piece(step)
        ref = arrived.at[kind, :, which]
        return remote(ref, ref, bc_send.at[step], bc_recv.at[step], other)

    def token_swap(kind):
        ref = tokens.at[kind, core]
        return remote(ref, ref, tk_send.at[kind], tk_recv.at[kind], other)

    def finish(kind):
        for step in ((0,) if kind == PROJECTED else (1, 2)):
            broadcast_all(step).wait_recv()
        position = lax.broadcasted_iota(jnp.int32, (1, span), 1)
        for e in range(seqs):
            total = part[kind, core, e] + sibling[kind, e]
            for k in range(NH - 1):
                total += arrived[kind, k, e].astype(F32)
            length = jnp.full((1, span), lens_s[0, e], jnp.int32)
            weight = (position < length).astype(F32) / length.astype(F32)
            tokens[kind, core, e] = (total * weight).astype(BF16)
        token_swap(kind).start()

    load_act.wait()
    small[0].wait()
    for e in range(seqs):
        projected = lax.dot_general(adapt[:, wc:], data[e, :, wc:], NT, preferred_element_type=F32)
        part[PROJECTED, 0, e] = projected[:half]
        part[PROJECTED, 1, e] = projected[half:]
    small[1].wait()

    def pull(e, _):
        load_cot(e).wait()
        pulled = lax.dot_general(adapt[:, :wc], data[e, :, :wc], NT, preferred_element_type=F32)
        part[PULLED, 0, e] = pulled[:half]
        part[PULLED, 1, e] = pulled[half:]

        @pl.when(e == mid - 1)
        def _():
            pl.semaphore_wait(barrier, len(peers))
            exchange(0).start()
            exchange(1).start()
            for peer in along_y:
                pl.semaphore_signal(plane_sem, inc=1, device_id=peer, device_id_type=MESH)

        @pl.when(e == mid)
        def _():
            broadcast(0)
            broadcast(1)

        return 0

    lax.fori_loop(0, seqs, pull, 0)
    exchange(2).start()
    pl.semaphore_wait(plane_sem, NY - 1)
    pl.semaphore_signal(all_sem, inc=1, device_id=(client(0, 1, 0), r), device_id_type=MESH)
    broadcast(2)
    small[2].wait()
    pl.semaphore_wait(all_sem, 1)

    def give_factors(k, _):
        to = target(k)
        p, j = to // PLANE, to % PLANE
        block, h = up_block(p, j), j % 2

        @pl.when(is_whole(p, j))
        def _():
            remote(adapt.at[:, lanes(block)], factors.at[rows(2 * k, 2)], a_send, a_recv, (to, r)).start()

        @pl.when(jnp.logical_not(is_whole(p, j)))
        def _():
            remote(adapt.at[rows(h, 1), lanes(block)], factors.at[rows(2 * k, 1)], a_send, a_recv, (to, r)).start()
            block2 = wc // LANES + down_block(p, j)
            remote(adapt.at[rows(h, 1), lanes(block2)], factors.at[rows(2 * k + 1, 1)], a_send, a_recv, (to, r)).start()

        return 0

    lax.fori_loop(0, OWNERS - 1, give_factors, 0)
    finish(PROJECTED)

    def fishers(kind, columns, width):
        total = jnp.zeros((rank, width), F32)
        for e in range(seqs):
            left = jnp.concatenate([tokens[kind, 0, e], tokens[kind, 1, e]], axis=0)
            grad = jnp.dot(left, data[e, :, columns], preferred_element_type=F32)
            total += grad * grad
        return total.astype(BF16)

    token_swap(PROJECTED).wait_recv()

    def up_stage(stage, _):
        @pl.when(stage == FINISH_AT)
        def _():
            finish(PULLED)

        p = lax.rem(x + pick(stage, 2, 1, 3, 0), NX)
        first = first_block(p)
        fisher = fishers(PROJECTED, pl.ds(pl.multiple_of(first * LANES, LANES), SPAN * LANES), SPAN * LANES)
        for b in range(SPAN):
            terms[stage, b * rank:(b + 1) * rank] = fisher[:, b * LANES:(b + 1) * LANES]

        def give(q, _):
            k = stage * PLANE + q
            to = target(k)
            j = to % PLANE
            unit = 2 * (up_block(p, j) - first)

            @pl.when(is_whole(p, j))
            def _():
                remote(terms.at[stage, rows(unit, 2)], fishers_in.at[rows(2 * k, 2)], f_send, f_recv, (to, r)).start()

            @pl.when(jnp.logical_not(is_whole(p, j)))
            def _():
                remote(terms.at[stage, rows(unit + j % 2, 1)], fishers_in.at[rows(2 * k, 1)], f_send, f_recv, (to, r)).start()

            return 0

        lax.fori_loop(0, jnp.where(stage == NX - 1, PLANE - 1, PLANE), give, 0)
        return 0

    lax.fori_loop(0, NX, up_stage, 0)

    token_swap(PULLED).wait_recv()
    fisher = fishers(PULLED, pl.ds(wc, wa), wa)
    for b in range(wa // LANES):
        dterms[b * rank:(b + 1) * rank] = fisher[:, b * LANES:(b + 1) * LANES]
    units = 2 * (wa // LANES)

    def give_down(k, _):
        n = lax.rem(c + k, units)
        to = jnp.minimum(n // 2, NX - 1) * PLANE + jnp.where(n < 6, 6 + n % 2, n - 2)

        @pl.when(c != to)
        def _():
            remote(dterms.at[rows(n, 1)], fishers_in.at[rows(2 * slot_at(to) + 1, 1)], f_send, f_recv, (to, r)).start()

        return 0

    lax.fori_loop(0, units, give_down, 0)

    j = c % PLANE
    whole = is_whole(x, j)
    unit = 2 * (up_block(x, j) - first_block(x))

    @pl.when(whole)
    def _():
        own[0] = terms[NX - 1, rows(unit, 2)]
        own[1] = adapt[:, lanes(up_block(x, j))]

    @pl.when(jnp.logical_not(whole))
    def _():
        block = down_block(x, j)
        own[0, :half] = terms[NX - 1, rows(unit + j % 2, 1)]
        own[0, half:] = dterms[rows(2 * block + j % 2, 1)]
        own[1, :half] = adapt[rows(j % 2, 1), lanes(up_block(x, j))]
        own[1, half:] = adapt[rows(j % 2, 1), lanes(wc // LANES + block)]

    remote(factors, factors, a_send, a_recv, other).wait_recv()
    remote(fishers_in, fishers_in, f_send, f_recv, other).wait_recv()
    total = own[0].astype(F32)
    weighted = total * own[1].astype(F32)

    def add(k, sums):
        fisher = fishers_in[rows(2 * k, 2)].astype(F32)
        return sums[0] + fisher, sums[1] + fisher * factors[rows(2 * k, 2)].astype(F32)

    total, weighted = lax.fori_loop(0, OWNERS - 1, add, (total, weighted), unroll=True)
    merged[...] = (weighted / (total + EPS)).astype(BF16)

    def publish(k, _):
        remote(merged, gathered.at[rows(2 * c, 2)], out_send, out_recv, (target(k), r)).start()
        return 0

    lax.fori_loop(0, OWNERS - 1, publish, 0)
    gathered[rows(2 * c, 2)] = merged[...]

    for step in range(3):
        exchange(step).wait_send()
        broadcast_all(step).wait_send()
    for kind in (PROJECTED, PULLED):
        token_swap(kind).wait_send()
    remote(factors, factors, a_send, a_recv, other).wait_send()
    remote(fishers_in, fishers_in, f_send, f_recv, other).wait_send()
    ref = gathered.at[pl.ds(0, rank * (OWNERS - 1))]
    remote(ref, ref, out_send, out_recv, other).wait()
    for owner in range(OWNERS):
        p, j = owner // PLANE, owner % PLANE
        h = j % 2
        if j < (6 if p < NX - 1 else 4):
            block = SPAN * p + j
            out[:, block * LANES:(block + 1) * LANES] = gathered[owner * rank:(owner + 1) * rank]
        else:
            block, dblock = (SPAN * p + 6, p) if p < NX - 1 else (25 + (j - 4) // 2, 3 + (j - 4) // 2)
            dblock += wc // LANES
            out[h * half:(h + 1) * half, block * LANES:(block + 1) * LANES] = gathered[owner * rank:owner * rank + half]
            out[h * half:(h + 1) * half, dblock * LANES:(dblock + 1) * LANES] = gathered[owner * rank + half:(owner + 1) * rank]


def local(*args):
    activations, cotangent, lengths, adapter_down, adapter_up = args
    _, seqs, span, wa = activations.shape
    wc = cotangent.shape[3]
    rank = adapter_down.shape[1]
    half = rank // 2
    width = wa + wc
    dma = pltpu.SemaphoreType.DMA
    out = pl.pallas_call(
        kernel,
        out_shape=jax.ShapeDtypeStruct((rank, width), BF16),
        in_specs=[pl.BlockSpec(memory_space=pl.ANY)] * 5,
        out_specs=pl.BlockSpec(memory_space=pltpu.VMEM),
        scratch_shapes=[
            pltpu.VMEM((seqs, span, width), BF16),
            pltpu.VMEM((rank, width), BF16),
            pltpu.SMEM((1, seqs), jnp.int32),
            pltpu.VMEM((2, 2, seqs, half, span), F32),
            pltpu.VMEM((2, seqs, half, span), F32),
            pltpu.VMEM((2, seqs, half, span), BF16),
            pltpu.VMEM((2, NH - 1, seqs, half, span), BF16),
            pltpu.VMEM((2, 2, seqs, half, span), BF16),
            pltpu.VMEM((NX, SPAN * rank, LANES), BF16),
            pltpu.VMEM((wa // LANES * rank, LANES), BF16),
            pltpu.VMEM((rank * (OWNERS - 1), LANES), BF16),
            pltpu.VMEM((rank * (OWNERS - 1), LANES), BF16),
            pltpu.VMEM((2, rank, LANES), BF16),
            pltpu.VMEM((rank, LANES), BF16),
            pltpu.VMEM((rank * OWNERS, LANES), BF16),
            dma((seqs + 1,)), dma((3,)), dma((3,)), dma((3,)), dma((3,)), dma((3,)), dma((2,)), dma((2,)),
            dma, dma, dma, dma, dma, dma, pltpu.SemaphoreType.REGULAR, pltpu.SemaphoreType.REGULAR,
        ],
        compiler_params=pltpu.CompilerParams(
            collective_id=0, has_side_effects=True, vmem_limit_bytes=48 * 1024 * 1024
        ),
    )(*(pltpu.with_memory_space_constraint(a, pltpu.HBM) for a in args))
    return out[:, wc:], out[:, :wc]


def solution(mesh):
    in_specs = (
        P("client", None, None, "row"),
        P("client", None, None, "row"),
        P("client", None),
        P("client", None, "row"),
        P("client", None, "row"),
    )
    out_specs = (P(None, "row"), P(None, "row"))
    return jax.shard_map(local, mesh=mesh, in_specs=in_specs, out_specs=out_specs, check_vma=False)
```

time: 37.3 us -> 35.2 us (0.944)
  Pallas kernels: 35.3 us -> 33.2 us
    pallas_call x1, Pallas kernels: 35.3 us -> 33.2 us  [local(): pl.pallas_call(kernel, out_shape=jax.ShapeDtypeStruct((rank, width), BF16...]
where the time goes in v3:
time: 35.2 us
  Pallas kernels  33.2 us (94%)
  local copies, waits for them, and re-layouts  1.32 us (4%)
  between operations  0.64 us (2%)
    pallas_call x1, Pallas kernels, local(): pl.pallas_call(kernel, out_shape=jax.ShapeDtypeStruct((rank, width), BF16...  33.2 us
    slice x2, local copies, waits for them, and re-layouts, local(): return (out[:, wc:], out[:, :wc])  1.32 us

profile of v3, /device:TPU:1, one launch (start us, length us, event | category | flops | bytes accessed | tf_op | source)
XLA Modules:
  0.0 35.2 jit_solution(1114918566586261803)
XLA Ops:
  0.6 33.2 %shard_map.68 = bf16[32,4096]{1,0:T(8,128)(2,1)S(1)} custom-call(bf16[1,4,256,640]{3,2,1,0:T(8,128)(2,1)} %act.1, bf16[1,4,256,3456]{3,2,1,0:T(8,128)(2,1)} %cot.1, s32[1,4]{1,0:T(1,128)} %lens.1, bf16[1,32,640]{2,1,0:T(8,128)(2,1)} %down.1, bf16[1,32,3456]{2,1,0:T(8,128)(2,1)} %up.1), custom_call_target="tpu_custom_call" | custom-call | tf_op jit(solution)/shard_map/pallas_call | solution.py:322
  33.8 0.6 %slice.6 = bf16[32,640]{1,0:T(8,128)(2,1)} slice(bf16[32,4096]{1,0:T(8,128)(2,1)S(1)} %shard_map.68), slice={[0:32], [3456:4096]} | slice | bytes 81920 | tf_op jit(solution)/shard_map/slice | solution.py:350
  34.5 0.7 %slice.7 = bf16[32,3456]{1,0:T(8,128)(2,1)} slice(bf16[32,4096]{1,0:T(8,128)(2,1)S(1)} %shard_map.68), slice={[0:32], [0:3456]} | slice | bytes 442368 | tf_op jit(solution)/shard_map/slice | solution.py:350

commit v4 on v3

--- a/solution.py
+++ b/solution.py
@@ -1,3 +1,7 @@
+import functools
+
+import functools
+
 import jax
 import jax.numpy as jnp
 from jax import lax
@@ -18,7 +22,9 @@
 UP_BLOCKS = 27
 SPAN = 7
 PROJECTED, PULLED = 0, 1
-FINISH_AT = 3
+FINISH_AT = 2
+SPLITS = (2, 2)
+FIRST = 3
 
 
 def pick(v, a, b, c, d):
@@ -35,7 +41,6 @@
     wc = cot.shape[3]
     rank = down.shape[1]
     half = rank // 2
-    mid = seqs // 2
     c = lax.axis_index("client")
     r = lax.axis_index("row")
     x, lo, y = c // PLANE, (c // NY) % NL, c % NY
@@ -47,7 +52,13 @@
     def chip(k):
         return (c, lax.rem(hi + k, NH) * NCORE + core)
 
+    xs = [lax.rem(x + d, NX) * PLANE for d in (2, 1, 3, 0)]
+    ls = [lax.rem(lo + d, NL) * NY for d in (1, 0)]
+    ys = [lax.rem(y + d, NY) for d in (2, 1, 3, 0)]
+
     def target(k):
+        if isinstance(k, int):
+            return xs[k // PLANE] + ls[k % PLANE // NY] + ys[k % NY]
         v, q = k // PLANE, k % PLANE
         return client(pick(v, 2, 1, 3, 0), 1 - q // NY, pick(q % NY, 2, 1, 3, 0))
 
@@ -88,20 +99,26 @@
     def load_cot(e):
         return pltpu.make_async_copy(cot.at[0, e], data.at[e, :, pl.ds(0, wc)], load_sem.at[e])
 
-    for copy in [small[0], load_act, small[1]] + [load_cot(e) for e in range(seqs)] + [small[2]]:
+    loads = [small[0], load_act, small[1]] + [load_cot(e) for e in range(seqs)] + [small[2]]
+    for copy in loads[:FIRST]:
         copy.start()
 
     barrier = pltpu.get_barrier_semaphore()
     for peer in peers:
         pl.semaphore_signal(barrier, inc=1, device_id=peer, device_id_type=MESH)
+    for copy in loads[FIRST:]:
+        copy.start()
 
     def remote(src, dst, send, recv, to):
         return pltpu.make_async_remote_copy(
             src_ref=src, dst_ref=dst, send_sem=send, recv_sem=recv, device_id=to, device_id_type=MESH
         )
 
+    ends = [sum(SPLITS[:i + 1]) for i in range(len(SPLITS))]
+    steps = 1 + len(SPLITS)
+
     def piece(step):
-        return (PROJECTED, pl.ds(0, seqs)) if step == 0 else (PULLED, pl.ds((step - 1) * mid, mid))
+        return (PROJECTED, pl.ds(0, seqs)) if step == 0 else (PULLED, pl.ds(ends[step - 1] - SPLITS[step - 1], SPLITS[step - 1]))
 
     def exchange(step):
         kind, which = piece(step)
@@ -124,7 +141,7 @@
         return remote(ref, ref, tk_send.at[kind], tk_recv.at[kind], other)
 
     def finish(kind):
-        for step in ((0,) if kind == PROJECTED else (1, 2)):
+        for step in ((0,) if kind == PROJECTED else range(1, steps)):
             broadcast_all(step).wait_recv()
         position = lax.broadcasted_iota(jnp.int32, (1, span), 1)
         for e in range(seqs):
@@ -136,6 +153,12 @@
             tokens[kind, core, e] = (total * weight).astype(BF16)
         token_swap(kind).start()
 
+    def meet():
+        pl.semaphore_wait(barrier, len(peers))
+        exchange(0).start()
+        for peer in along_y:
+            pl.semaphore_signal(plane_sem, inc=1, device_id=peer, device_id_type=MESH)
+
     load_act.wait()
     small[0].wait()
     for e in range(seqs):
@@ -150,32 +173,38 @@
         part[PULLED, 0, e] = pulled[:half]
         part[PULLED, 1, e] = pulled[half:]
 
-        @pl.when(e == mid - 1)
-        def _():
-            pl.semaphore_wait(barrier, len(peers))
-            exchange(0).start()
-            exchange(1).start()
-            for peer in along_y:
-                pl.semaphore_signal(plane_sem, inc=1, device_id=peer, device_id_type=MESH)
-
-        @pl.when(e == mid)
-        def _():
-            broadcast(0)
-            broadcast(1)
-
+        pl.when(e == 0)(meet)
+
+        for step in range(1, steps):
+            pl.when(e == sent_at[step])(exchange(step).start)
+        for step in range(steps):
+            if cast_at[step] < seqs:
+                pl.when(e == cast_at[step])(functools.partial(broadcast, step))
         return 0
 
+    sent_at = [0] + [end - 1 for end in ends]
+    cast_at = [0] + [end for end in ends]
     lax.fori_loop(0, seqs, pull, 0)
-    exchange(2).start()
+    for step in range(steps):
+        if cast_at[step] >= seqs:
+            broadcast(step)
     pl.semaphore_wait(plane_sem, NY - 1)
     pl.semaphore_signal(all_sem, inc=1, device_id=(client(0, 1, 0), r), device_id_type=MESH)
-    broadcast(2)
     small[2].wait()
-    pl.semaphore_wait(all_sem, 1)
-
-    def give_factors(k, _):
-        to = target(k)
-        p, j = to // PLANE, to % PLANE
+
+    def give_factors(v, _):
+        p = lax.rem(x + pick(v, 2, 1, 3, 0), NX)
+        for q in range(PLANE):
+            if q < PLANE - 1:
+                give_factor(v, p, q)
+            else:
+                pl.when(v < NX - 1)(functools.partial(give_factor, v, p, q))
+        return 0
+
+    def give_factor(v, p, q):
+        k = v * PLANE + q
+        j = ls[q // NY] + ys[q % NY]
+        to = p * PLANE + j
         block, h = up_block(p, j), j % 2
 
         @pl.when(is_whole(p, j))
@@ -188,9 +217,9 @@
             block2 = wc // LANES + down_block(p, j)
             remote(adapt.at[rows(h, 1), lanes(block2)], factors.at[rows(2 * k + 1, 1)], a_send, a_recv, (to, r)).start()
 
-        return 0
-
-    lax.fori_loop(0, OWNERS - 1, give_factors, 0)
+
+    pl.semaphore_wait(all_sem, 1)
+    lax.fori_loop(0, NX, give_factors, 0)
     finish(PROJECTED)
 
     def fishers(kind, columns, width):
@@ -203,6 +232,26 @@
 
     token_swap(PROJECTED).wait_recv()
 
+    units = 2 * (wa // LANES)
+
+    def down_stage():
+        token_swap(PULLED).wait_recv()
+        fisher = fishers(PULLED, pl.ds(wc, wa), wa)
+        for b in range(wa // LANES):
+            dterms[b * rank:(b + 1) * rank] = fisher[:, b * LANES:(b + 1) * LANES]
+
+        def give_down(k, _):
+            n = lax.rem(c + k, units)
+            to = jnp.minimum(n // 2, NX - 1) * PLANE + jnp.where(n < 6, 6 + n % 2, n - 2)
+
+            @pl.when(c != to)
+            def _():
+                remote(dterms.at[rows(n, 1)], fishers_in.at[rows(2 * slot_at(to) + 1, 1)], f_send, f_recv, (to, r)).start()
+
+            return 0
+
+        lax.fori_loop(0, units, give_down, 0)
+
     def up_stage(stage, _):
         @pl.when(stage == FINISH_AT)
         def _():
@@ -214,10 +263,10 @@
         for b in range(SPAN):
             terms[stage, b * rank:(b + 1) * rank] = fisher[:, b * LANES:(b + 1) * LANES]
 
-        def give(q, _):
+        def give(q):
             k = stage * PLANE + q
-            to = target(k)
-            j = to % PLANE
+            j = ls[q // NY] + ys[q % NY]
+            to = p * PLANE + j
             unit = 2 * (up_block(p, j) - first)
 
             @pl.when(is_whole(p, j))
@@ -228,30 +277,16 @@
             def _():
                 remote(terms.at[stage, rows(unit + j % 2, 1)], fishers_in.at[rows(2 * k, 1)], f_send, f_recv, (to, r)).start()
 
-            return 0
-
-        lax.fori_loop(0, jnp.where(stage == NX - 1, PLANE - 1, PLANE), give, 0)
+        for q in range(PLANE):
+            if q < PLANE - 1:
+                give(q)
+            else:
+                pl.when(stage < NX - 1)(functools.partial(give, q))
         return 0
 
     lax.fori_loop(0, NX, up_stage, 0)
 
-    token_swap(PULLED).wait_recv()
-    fisher = fishers(PULLED, pl.ds(wc, wa), wa)
-    for b in range(wa // LANES):
-        dterms[b * rank:(b + 1) * rank] = fisher[:, b * LANES:(b + 1) * LANES]
-    units = 2 * (wa // LANES)
-
-    def give_down(k, _):
-        n = lax.rem(c + k, units)
-        to = jnp.minimum(n // 2, NX - 1) * PLANE + jnp.where(n < 6, 6 + n % 2, n - 2)
-
-        @pl.when(c != to)
-        def _():
-            remote(dterms.at[rows(n, 1)], fishers_in.at[rows(2 * slot_at(to) + 1, 1)], f_send, f_recv, (to, r)).start()
-
-        return 0
-
-    lax.fori_loop(0, units, give_down, 0)
+    down_stage()
 
     j = c % PLANE
     whole = is_whole(x, j)
@@ -286,10 +321,11 @@
         remote(merged, gathered.at[rows(2 * c, 2)], out_send, out_recv, (target(k), r)).start()
         return 0
 
-    lax.fori_loop(0, OWNERS - 1, publish, 0)
+    for k in range(OWNERS - 1):
+        publish(k, 0)
     gathered[rows(2 * c, 2)] = merged[...]
 
-    for step in range(3):
+    for step in range(steps):
         exchange(step).wait_send()
         broadcast_all(step).wait_send()
     for kind in (PROJECTED, PULLED):

time: 35.2 us -> 33.4 us (0.949)
  Pallas kernels: 33.2 us -> 31.3 us
    pallas_call x1, Pallas kernels: 33.2 us -> 31.3 us  [local(): pl.pallas_call(kernel, out_shape=jax.ShapeDtypeStruct((rank, width), BF16...]
where the time goes in v4:
time: 33.4 us; the launch traced here: 33.3 us
  Pallas kernels  31.3 us (94%)
  local copies, waits for them, and re-layouts  1.32 us (4%)
  between operations  0.64 us (2%)
    pallas_call x1, Pallas kernels, local(): pl.pallas_call(kernel, out_shape=jax.ShapeDtypeStruct((rank, width), BF16...  31.3 us
    slice x2, local copies, waits for them, and re-layouts, local(): return (out[:, wc:], out[:, :wc])  1.32 us

profile of v4, /device:TPU:1, one launch (start us, length us, event | category | flops | bytes accessed | tf_op | source)
XLA Modules:
  0.0 33.3 jit_solution(10406885070742671651)
XLA Ops:
  0.6 31.3 %shard_map.68 = bf16[32,4096]{1,0:T(8,128)(2,1)S(1)} custom-call(bf16[1,4,256,640]{3,2,1,0:T(8,128)(2,1)} %act.1, bf16[1,4,256,3456]{3,2,1,0:T(8,128)(2,1)} %cot.1, s32[1,4]{1,0:T(1,128)} %lens.1, bf16[1,32,640]{2,1,0:T(8,128)(2,1)} %down.1, bf16[1,32,3456]{2,1,0:T(8,128)(2,1)} %up.1), custom_call_target="tpu_custom_call" | custom-call | tf_op jit(solution)/shard_map/pallas_call | solution.py:358
  32.0 0.6 %slice.6 = bf16[32,640]{1,0:T(8,128)(2,1)} slice(bf16[32,4096]{1,0:T(8,128)(2,1)S(1)} %shard_map.68), slice={[0:32], [3456:4096]} | slice | bytes 81920 | tf_op jit(solution)/shard_map/slice | solution.py:386
  32.6 0.7 %slice.7 = bf16[32,3456]{1,0:T(8,128)(2,1)} slice(bf16[32,4096]{1,0:T(8,128)(2,1)S(1)} %shard_map.68), slice={[0:32], [0:3456]} | slice | bytes 442368 | tf_op jit(solution)/shard_map/slice | solution.py:386

commit v5 on v4

--- a/solution.py
+++ b/solution.py
@@ -27,6 +27,10 @@
 FIRST = 3
 
 
+def hops(offset):
+    return sum(min(d, n - d) for d, n in zip(offset, (NX, NL, NY)))
+
+
 def pick(v, a, b, c, d):
     return jnp.where(v == 0, a, jnp.where(v == 1, b, jnp.where(v == 2, c, d)))
 
@@ -317,12 +321,12 @@
     total, weighted = lax.fori_loop(0, OWNERS - 1, add, (total, weighted), unroll=True)
     merged[...] = (weighted / (total + EPS)).astype(BF16)
 
-    def publish(k, _):
-        remote(merged, gathered.at[rows(2 * c, 2)], out_send, out_recv, (target(k), r)).start()
-        return 0
-
-    for k in range(OWNERS - 1):
-        publish(k, 0)
+    def publish(to):
+        remote(merged, gathered.at[rows(2 * c, 2)], out_send, out_recv, (to, r)).start()
+
+    offsets = [(dx, dl, dy) for dx in range(NX) for dl in range(NL) for dy in range(NY)][1:]
+    for offset in sorted(offsets, key=lambda o: (-hops(o), (o[0] + o[2]) % 4, o[1])):
+        publish(client(*offset))
     gathered[rows(2 * c, 2)] = merged[...]
 
     for step in range(steps):

time: 33.4 us -> 33.3 us (level)
  no operation moved by 1% of the time
where the time goes in v5:
time: 33.3 us; the launch traced here: 33.2 us
  Pallas kernels  31.2 us (94%)
  local copies, waits for them, and re-layouts  1.32 us (4%)
  between operations  0.64 us (2%)
    pallas_call x1, Pallas kernels, local(): pl.pallas_call(kernel, out_shape=jax.ShapeDtypeStruct((rank, width), BF16...  31.2 us
    slice x2, local copies, waits for them, and re-layouts, local(): return (out[:, wc:], out[:, :wc])  1.32 us

profile of v5, /device:TPU:1, one launch (start us, length us, event | category | flops | bytes accessed | tf_op | source)
XLA Modules:
  0.0 33.2 jit_solution(9187756996215444054)
XLA Ops:
  0.6 31.2 %shard_map.68 = bf16[32,4096]{1,0:T(8,128)(2,1)S(1)} custom-call(bf16[1,4,256,640]{3,2,1,0:T(8,128)(2,1)} %act.1, bf16[1,4,256,3456]{3,2,1,0:T(8,128)(2,1)} %cot.1, s32[1,4]{1,0:T(1,128)} %lens.1, bf16[1,32,640]{2,1,0:T(8,128)(2,1)} %down.1, bf16[1,32,3456]{2,1,0:T(8,128)(2,1)} %up.1), custom_call_target="tpu_custom_call" | custom-call | tf_op jit(solution)/shard_map/pallas_call | solution.py:362
  31.9 0.6 %slice.6 = bf16[32,640]{1,0:T(8,128)(2,1)} slice(bf16[32,4096]{1,0:T(8,128)(2,1)S(1)} %shard_map.68), slice={[0:32], [3456:4096]} | slice | bytes 81920 | tf_op jit(solution)/shard_map/slice | solution.py:390
  32.5 0.7 %slice.7 = bf16[32,3456]{1,0:T(8,128)(2,1)} slice(bf16[32,4096]{1,0:T(8,128)(2,1)S(1)} %shard_map.68), slice={[0:32], [0:3456]} | slice | bytes 442368 | tf_op jit(solution)/shard_map/slice | solution.py:390

commit v6 on v5

--- a/solution.py
+++ b/solution.py
@@ -250,7 +250,7 @@
 
             @pl.when(c != to)
             def _():
-                remote(dterms.at[rows(n, 1)], fishers_in.at[rows(2 * slot_at(to) + 1, 1)], f_send, f_recv, (to, r)).start()
+                remote(dterms.at[rows(n, 1)], fishers_in.at[rows(2 * slot_at(to) + 1, 1)], f_send, f_recv.at[1], (to, r)).start()
 
             return 0
 
@@ -275,11 +275,11 @@
 
             @pl.when(is_whole(p, j))
             def _():
-                remote(terms.at[stage, rows(unit, 2)], fishers_in.at[rows(2 * k, 2)], f_send, f_recv, (to, r)).start()
+                remote(terms.at[stage, rows(unit, 2)], fishers_in.at[rows(2 * k, 2)], f_send, f_recv.at[stage // (NX - 1)], (to, r)).start()
 
             @pl.when(jnp.logical_not(is_whole(p, j)))
             def _():
-                remote(terms.at[stage, rows(unit + j % 2, 1)], fishers_in.at[rows(2 * k, 1)], f_send, f_recv, (to, r)).start()
+                remote(terms.at[stage, rows(unit + j % 2, 1)], fishers_in.at[rows(2 * k, 1)], f_send, f_recv.at[stage // (NX - 1)], (to, r)).start()
 
         for q in range(PLANE):
             if q < PLANE - 1:
@@ -310,15 +310,32 @@
         own[1, half:] = adapt[rows(j % 2, 1), lanes(wc // LANES + block)]
 
     remote(factors, factors, a_send, a_recv, other).wait_recv()
-    remote(fishers_in, fishers_in, f_send, f_recv, other).wait_recv()
-    total = own[0].astype(F32)
-    weighted = total * own[1].astype(F32)
-
-    def add(k, sums):
-        fisher = fishers_in[rows(2 * k, 2)].astype(F32)
-        return sums[0] + fisher, sums[1] + fisher * factors[rows(2 * k, 2)].astype(F32)
-
-    total, weighted = lax.fori_loop(0, OWNERS - 1, add, (total, weighted), unroll=True)
+    early = PLANE * (NX - 1)
+
+    def await_units(n, which):
+        ref = fishers_in.at[pl.ds(0, n * half)]
+        remote(ref, ref, f_send, f_recv.at[which], other).wait_recv()
+
+    def sums(at, start, stop, n):
+        total = own[0, at:at + n].astype(F32)
+        return add(total, total * own[1, at:at + n].astype(F32), at, start, stop, n)
+
+    def add(total, weighted, at, start, stop, n):
+        for k in range(start, stop):
+            here = pl.ds(k * rank + at, n)
+            fisher = fishers_in[here].astype(F32)
+            total += fisher
+            weighted += fisher * factors[here].astype(F32)
+        return total, weighted
+
+    pl.when(whole)(functools.partial(await_units, 2 * early, 0))
+    pl.when(jnp.logical_not(whole))(functools.partial(await_units, early, 0))
+    top = sums(0, 0, early, half)
+    pl.when(whole)(functools.partial(await_units, 2 * (OWNERS - 1 - early), 1))
+    pl.when(jnp.logical_not(whole))(functools.partial(await_units, 2 * (OWNERS - 1) - early, 1))
+    top = add(*top, 0, early, OWNERS - 1, half)
+    bottom = sums(half, 0, OWNERS - 1, half)
+    total, weighted = (jnp.concatenate(pair_of, axis=0) for pair_of in zip(top, bottom))
     merged[...] = (weighted / (total + EPS)).astype(BF16)
 
     def publish(to):
@@ -335,7 +352,7 @@
     for kind in (PROJECTED, PULLED):
         token_swap(kind).wait_send()
     remote(factors, factors, a_send, a_recv, other).wait_send()
-    remote(fishers_in, fishers_in, f_send, f_recv, other).wait_send()
+    remote(fishers_in, fishers_in, f_send, f_recv.at[0], other).wait_send()
     ref = gathered.at[pl.ds(0, rank * (OWNERS - 1))]
     remote(ref, ref, out_send, out_recv, other).wait()
     for owner in range(OWNERS):
@@ -381,7 +398,7 @@
             pltpu.VMEM((rank, LANES), BF16),
             pltpu.VMEM((rank * OWNERS, LANES), BF16),
             dma((seqs + 1,)), dma((3,)), dma((3,)), dma((3,)), dma((3,)), dma((3,)), dma((2,)), dma((2,)),
-            dma, dma, dma, dma, dma, dma, pltpu.SemaphoreType.REGULAR, pltpu.SemaphoreType.REGULAR,
+            dma, dma, dma, dma((2,)), dma, dma, pltpu.SemaphoreType.REGULAR, pltpu.SemaphoreType.REGULAR,
         ],
         compiler_params=pltpu.CompilerParams(
             collective_id=0, has_side_effects=True, vmem_limit_bytes=48 * 1024 * 1024

time: 33.3 us -> 33.3 us (level)
  no operation moved by 1% of the time
where the time goes in v6:
time: 33.3 us; the launch traced here: 33.2 us
  Pallas kernels  31.2 us (94%)
  local copies, waits for them, and re-layouts  1.32 us (4%)
  between operations  0.64 us (2%)
    pallas_call x1, Pallas kernels, local(): pl.pallas_call(kernel, out_shape=jax.ShapeDtypeStruct((rank, width), BF16...  31.2 us
    slice x2, local copies, waits for them, and re-layouts, local(): return (out[:, wc:], out[:, :wc])  1.32 us

profile of v6, /device:TPU:1, one launch (start us, length us, event | category | flops | bytes accessed | tf_op | source)
XLA Modules:
  0.0 33.2 jit_solution(9898325833008921831)
XLA Ops:
  0.6 31.2 %shard_map.68 = bf16[32,4096]{1,0:T(8,128)(2,1)S(1)} custom-call(bf16[1,4,256,640]{3,2,1,0:T(8,128)(2,1)} %act.1, bf16[1,4,256,3456]{3,2,1,0:T(8,128)(2,1)} %cot.1, s32[1,4]{1,0:T(1,128)} %lens.1, bf16[1,32,640]{2,1,0:T(8,128)(2,1)} %down.1, bf16[1,32,3456]{2,1,0:T(8,128)(2,1)} %up.1), custom_call_target="tpu_custom_call" | custom-call | tf_op jit(solution)/shard_map/pallas_call | solution.py:379
  31.9 0.6 %slice.6 = bf16[32,640]{1,0:T(8,128)(2,1)} slice(bf16[32,4096]{1,0:T(8,128)(2,1)S(1)} %shard_map.68), slice={[0:32], [3456:4096]} | slice | bytes 81920 | tf_op jit(solution)/shard_map/slice | solution.py:407
  32.5 0.7 %slice.7 = bf16[32,3456]{1,0:T(8,128)(2,1)} slice(bf16[32,4096]{1,0:T(8,128)(2,1)S(1)} %shard_map.68), slice={[0:32], [0:3456]} | slice | bytes 442368 | tf_op jit(solution)/shard_map/slice | solution.py:407

commit v7 on v6

--- a/solution.py
+++ b/solution.py
@@ -22,7 +22,7 @@
 UP_BLOCKS = 27
 SPAN = 7
 PROJECTED, PULLED = 0, 1
-FINISH_AT = 2
+FINISH_AT = 3
 SPLITS = (2, 2)
 FIRST = 3
 

time: 33.3 us -> 33.3 us (level)
  no operation moved by 1% of the time
where the time goes in v7:
time: 33.3 us; the launch traced here: 33.2 us
  Pallas kernels  31.2 us (94%)
  local copies, waits for them, and re-layouts  1.32 us (4%)
  between operations  0.64 us (2%)
    pallas_call x1, Pallas kernels, local(): pl.pallas_call(kernel, out_shape=jax.ShapeDtypeStruct((rank, width), BF16...  31.2 us
    slice x2, local copies, waits for them, and re-layouts, local(): return (out[:, wc:], out[:, :wc])  1.32 us

profile of v7, /device:TPU:1, one launch (start us, length us, event | category | flops | bytes accessed | tf_op | source)
XLA Modules:
  0.0 33.2 jit_solution(17749407731291507141)
XLA Ops:
  0.6 31.2 %shard_map.68 = bf16[32,4096]{1,0:T(8,128)(2,1)S(1)} custom-call(bf16[1,4,256,640]{3,2,1,0:T(8,128)(2,1)} %act.1, bf16[1,4,256,3456]{3,2,1,0:T(8,128)(2,1)} %cot.1, s32[1,4]{1,0:T(1,128)} %lens.1, bf16[1,32,640]{2,1,0:T(8,128)(2,1)} %down.1, bf16[1,32,3456]{2,1,0:T(8,128)(2,1)} %up.1), custom_call_target="tpu_custom_call" | custom-call | tf_op jit(solution)/shard_map/pallas_call | solution.py:379
  31.9 0.6 %slice.6 = bf16[32,640]{1,0:T(8,128)(2,1)} slice(bf16[32,4096]{1,0:T(8,128)(2,1)S(1)} %shard_map.68), slice={[0:32], [3456:4096]} | slice | bytes 81920 | tf_op jit(solution)/shard_map/slice | solution.py:407
  32.5 0.7 %slice.7 = bf16[32,3456]{1,0:T(8,128)(2,1)} slice(bf16[32,4096]{1,0:T(8,128)(2,1)S(1)} %shard_map.68), slice={[0:32], [0:3456]} | slice | bytes 442368 | tf_op jit(solution)/shard_map/slice | solution.py:407
